TPU v7x, 32 devices: a whole 2x2x4 slice. The times are simulated.
32 devices in a mesh: freq: 8 (over z, y), sta: 4 (over x, core).
Axes of the slice: x: 2, y: 2, z: 4, core: 2. Of those that a mesh axis runs over, the one named last changes fastest.
Arguments:
- spectra: float32 [2, 128, 64, 8192], P(None, 'freq', None, 'sta'), may hold values from -24 to 24
- current: float32 [64, 2, 128, 512], P('freq', None, None, 'sta'), may hold values from -600 to 600, as said below
- previous: float32 [64, 2, 128, 512], P('freq', None, None, 'sta'), may hold values from -600 to 600, as said below
- table: int32 [64, 512], replicated, may hold values from 0 to 16383
- station_block: int32 [8192], P('sta'), may hold values from 0 to 63
- offsets: float32 [2, 8192], P(None, 'sta'), may hold values from -4 to 4
- slowness: float32 [2, 512], replicated, may hold values from -3 to 3
- weights: float32 [512], P('sta'), may hold values from 400 to 5000
- momentum: float32 [1], replicated, may hold values from 2 to 10
Outputs:
- estimate: float32 [64, 2, 128, 512], P('freq', None, None, 'sta')
- extrapolated: float32 [64, 2, 128, 512], P('freq', None, None, 'sta')
Inputs may be any that keep to these rules, and one draw needn't show every extreme that they name: `current`: real values. `previous`: real values.
All inputs are finite; a program needn't handle non-finite values.
Results may differ from a plain program's by a relative error of at most 0.00105.
The roundings to bfloat16 on the way count: a program that leaves them out, or rounds other values in their place, can miss the bound.
Values may be sent and summed in bfloat16 or wider, within the bound.
A program may use at most 192 MiB of HBM per device.

v0:
```python
import math
import jax
import jax.numpy as jnp
from jax import lax
from jax.sharding import PartitionSpec as P

F = 64
CELLS = 512


def cell_block(cell_count):
    block_len = cell_count
    while block_len > 512 and block_len % 2 == 0:
        block_len = block_len // 2
    return block_len


def phases(number, delay_rows, off_rows, slow_cols, period):
    wrapped = number * delay_rows % period
    geometry = (
        off_rows[0][:, None] * slow_cols[0][None, :] + off_rows[1][:, None] * slow_cols[1][None, :]
    )
    phase_angle = (wrapped.astype(jnp.float32) + number.astype(jnp.float32) * geometry) * (
        2.0 * math.pi / period
    )
    return (jnp.cos(phase_angle).astype(jnp.bfloat16), jnp.sin(phase_angle).astype(jnp.bfloat16))


def forward_terms(cos_part, sin_part, iterate):
    window_count = iterate.shape[1]
    stacked = iterate.reshape(2 * window_count, iterate.shape[2])
    contract = (((1,), (1,)), ((), ()))
    with_cos = lax.dot_general(stacked, cos_part, contract, preferred_element_type=jnp.float32)
    with_sin = lax.dot_general(stacked, sin_part, contract, preferred_element_type=jnp.float32)
    real_part = with_cos[:window_count] + with_sin[window_count:]
    imag_part = with_cos[window_count:] - with_sin[:window_count]
    return jnp.stack([real_part, imag_part])


def adjoint_terms(cos_part, sin_part, residual):
    window_count = residual.shape[1]
    stacked = residual.reshape(2 * window_count, residual.shape[2])
    with_cos = jnp.dot(stacked, cos_part, preferred_element_type=jnp.float32)
    with_sin = jnp.dot(stacked, sin_part, preferred_element_type=jnp.float32)
    real_part = with_cos[:window_count] - with_sin[window_count:]
    imag_part = with_cos[window_count:] + with_sin[:window_count]
    return jnp.stack([real_part, imag_part])


def local(spectra, current, previous, table, station_block, offsets, slowness, weights, momentum):
    period = 4 * F
    normalizer = 1.0 / math.sqrt(CELLS)
    bin_count = current.shape[0]
    cell_share = current.shape[3]
    stations_here = station_block.shape[0]
    station_total = stations_here * lax.axis_size("sta")
    first_bin = lax.axis_index("freq") * bin_count
    relaid = lax.all_to_all(
        spectra.astype(jnp.bfloat16), "freq", split_axis=2, concat_axis=1, tiled=True
    ).astype(spectra.dtype)
    iterate_b = current.astype(jnp.bfloat16)
    segment = lax.all_gather(iterate_b, "sta", axis=3, tiled=True)
    cell_count = segment.shape[3]
    block_len = cell_block(cell_count)
    delay_rows = jnp.take(table, station_block, axis=0)
    bin_terms = []
    cos_blocks = []
    sin_blocks = []
    for add_bin_index in range(bin_count):
        cos_part, sin_part = phases(
            first_bin + add_bin_index + 1, delay_rows, offsets, slowness, period
        )
        cos_blocks.append(cos_part)
        sin_blocks.append(sin_part)
        bin_terms.append(
            forward_terms(cos_part, sin_part, segment[add_bin_index, :, :, 0:block_len])
        )
    running = jnp.stack(bin_terms)
    cos_all = jnp.stack(cos_blocks)
    sin_all = jnp.stack(sin_blocks)
    predicted, cos_all, sin_all = (running, cos_all, sin_all)
    bin_sums = []
    for bin_index in range(bin_count):
        residual = (predicted[bin_index] * normalizer - relaid[:, :, bin_index, :]).astype(
            jnp.bfloat16
        )
        bin_sums.append(
            adjoint_terms(cos_all[bin_index], sin_all[bin_index], residual) * normalizer
        )
    partial_sums = jnp.stack(bin_sums)
    summed = lax.psum(partial_sums, "sta")
    gradient = lax.dynamic_slice_in_dim(summed, lax.axis_index("sta") * cell_share, cell_share, 3)
    step_size = CELLS / (math.sqrt(station_total) + math.sqrt(CELLS)) ** 2
    stepped = current - step_size * gradient
    threshold = step_size * weights
    squares = jnp.sum(stepped * stepped, axis=(0, 1))
    group_norm = jnp.sqrt(lax.psum(squares, "freq") + 1e-06)
    estimate = stepped * jnp.maximum(0.0, 1.0 - threshold[None, :] / group_norm)
    momentum_now = momentum[0]
    momentum_next = (1.0 + jnp.sqrt(1.0 + 4.0 * momentum_now * momentum_now)) / 2.0
    extrapolated = estimate + (momentum_now - 1.0) / momentum_next * (estimate - previous)
    return (estimate, extrapolated)


def solution(mesh):
    in_specs = (
        P(None, "freq", None, "sta"),
        P("freq", None, None, "sta"),
        P("freq", None, None, "sta"),
        P(),
        P("sta"),
        P(None, "sta"),
        P(),
        P("sta"),
        P(),
    )
    out_specs = (P("freq", None, None, "sta"), P("freq", None, None, "sta"))
    return jax.shard_map(local, mesh=mesh, in_specs=in_specs, out_specs=out_specs, check_vma=False)
```

profile of v0, /device:TPU:0, one launch (start us, length us, event | category | flops | bytes accessed | tf_op | source)
XLA Modules:
  0.0 836.7 jit_solution(6741037382420943036)
XLA Ops:
  9.4 17.2 %copy.25 = bf16[2,16,64,2048]{3,1,0,2:T(8,128)(2,1)} copy(f32[2,16,64,2048]{3,2,1,0:T(8,128)} %param.9) | data formatting | bytes 25165824 | tf_op args[0]
  43.6 18.0 %fusion.31 = (f32[2048,512]{1,0:T(8,128)}, f32[2048,512]{1,0:T(8,128)}, f32[2048,512]{1,0:T(8,128)}, f32[2048,512]{1,0:T(8,128)}, f32[2048,512]{1,0:T(8,128)}, /*index=5*/f32[2048,512]{1,0:T(8,128)}) fusion(s32[2048,512]{1,0:T(8,128)} %gather_fusion, f32[]{:T(128)S(6)} %convert_element_type.188, s32[]{:T(128)S(6)} %add.230, f32[512]{0:T(512)S(1)} %bitcast.221, ...), kind=kLoop, calls=%fused_computation.58 | loop fusion | flops 104857600 | bytes 29382704 | tf_op jit(solution)/shard_map/mul | solution.py:23
  73.1 15.0 %convolution_bitcast_fusion.2 = f32[256,2048]{1,0:T(8,128)S(1)} fusion(bf16[256,512]{1,0:T(8,128)(2,1)S(1)} %bitcast.213, f32[2048,512]{1,0:T(8,128)S(1)} %copy-done.16), kind=kOutput, calls=%fused_computation.78 | convolution fusion | flops 537919488 | bytes 6553600 | tf_op jit(solution)/shard_map/dot_general | solution.py:34
  88.2 14.9 %convolution_bitcast_fusion.3 = f32[256,2048]{1,0:T(8,128)S(1)} fusion(bf16[256,512]{1,0:T(8,128)(2,1)S(1)} %bitcast.214, f32[2048,512]{1,0:T(8,128)S(1)} %copy-done.16), kind=kOutput, calls=%fused_computation.79 | convolution fusion | flops 537919488 | bytes 6553600 | tf_op jit(solution)/shard_map/dot_general | solution.py:33
  106.0 15.0 %convolution_bitcast_fusion.14 = f32[256,2048]{1,0:T(8,128)S(1)} fusion(bf16[256,512]{1,0:T(8,128)(2,1)S(1)} %bitcast.211, f32[2048,512]{1,0:T(8,128)S(1)} %copy-done.14), kind=kOutput, calls=%fused_computation.90 | convolution fusion | flops 537919488 | bytes 6553600 | tf_op jit(solution)/shard_map/dot_general | solution.py:34
  121.0 15.1 %convolution_bitcast_fusion.15 = f32[256,2048]{1,0:T(8,128)S(1)} fusion(bf16[256,512]{1,0:T(8,128)(2,1)S(1)} %bitcast.212, f32[2048,512]{1,0:T(8,128)S(1)} %copy-done.14), kind=kOutput, calls=%fused_computation.91 | convolution fusion | flops 537919488 | bytes 6553600 | tf_op jit(solution)/shard_map/dot_general | solution.py:33
  137.9 15.0 %convolution_bitcast_fusion = f32[256,2048]{1,0:T(8,128)S(1)} fusion(bf16[256,512]{1,0:T(8,128)(2,1)S(1)} %bitcast.209, f32[2048,512]{1,0:T(8,128)S(1)} %copy-done.12), kind=kOutput, calls=%fused_computation.76 | convolution fusion | flops 537919488 | bytes 6553600 | tf_op jit(solution)/shard_map/dot_general | solution.py:34
  152.9 14.9 %convolution_bitcast_fusion.1 = f32[256,2048]{1,0:T(8,128)S(1)} fusion(bf16[256,512]{1,0:T(8,128)(2,1)S(1)} %bitcast.210, f32[2048,512]{1,0:T(8,128)S(1)} %copy-done.12), kind=kOutput, calls=%fused_computation.77 | convolution fusion | flops 537919488 | bytes 6553600 | tf_op jit(solution)/shard_map/dot_general | solution.py:33
  169.9 15.0 %convolution_bitcast_fusion.12 = f32[256,2048]{1,0:T(8,128)S(1)} fusion(bf16[256,512]{1,0:T(8,128)(2,1)S(1)} %bitcast.207, f32[2048,512]{1,0:T(8,128)S(1)} %copy-done.10), kind=kOutput, calls=%fused_computation.88 | convolution fusion | flops 537919488 | bytes 6553600 | tf_op jit(solution)/shard_map/dot_general | solution.py:34
  184.9 14.9 %convolution_bitcast_fusion.13 = f32[256,2048]{1,0:T(8,128)S(1)} fusion(bf16[256,512]{1,0:T(8,128)(2,1)S(1)} %bitcast.208, f32[2048,512]{1,0:T(8,128)S(1)} %copy-done.10), kind=kOutput, calls=%fused_computation.89 | convolution fusion | flops 537919488 | bytes 6553600 | tf_op jit(solution)/shard_map/dot_general | solution.py:33
  201.6 15.2 %convolution_bitcast_fusion.10 = f32[256,2048]{1,0:T(8,128)S(1)} fusion(bf16[256,512]{1,0:T(8,128)(2,1)S(1)} %bitcast.205, f32[2048,512]{1,0:T(8,128)S(1)} %copy-done.8), kind=kOutput, calls=%fused_computation.86 | convolution fusion | flops 537919488 | bytes 6553600 | tf_op jit(solution)/shard_map/dot_general | solution.py:34
  216.8 14.9 %convolution_bitcast_fusion.11 = f32[256,2048]{1,0:T(8,128)S(1)} fusion(bf16[256,512]{1,0:T(8,128)(2,1)S(1)} %bitcast.206, f32[2048,512]{1,0:T(8,128)S(1)} %copy-done.8), kind=kOutput, calls=%fused_computation.87 | convolution fusion | flops 537919488 | bytes 6553600 | tf_op jit(solution)/shard_map/dot_general | solution.py:33
  233.6 15.0 %convolution_bitcast_fusion.8 = f32[256,2048]{1,0:T(8,128)S(1)} fusion(bf16[256,512]{1,0:T(8,128)(2,1)S(1)} %bitcast.203, f32[2048,512]{1,0:T(8,128)S(1)} %copy-done.6), kind=kOutput, calls=%fused_computation.84 | convolution fusion | flops 537919488 | bytes 6553600 | tf_op jit(solution)/shard_map/dot_general | solution.py:34
  248.6 14.9 %convolution_bitcast_fusion.9 = f32[256,2048]{1,0:T(8,128)S(1)} fusion(bf16[256,512]{1,0:T(8,128)(2,1)S(1)} %bitcast.204, f32[2048,512]{1,0:T(8,128)S(1)} %copy-done.6), kind=kOutput, calls=%fused_computation.85 | convolution fusion | flops 537919488 | bytes 6553600 | tf_op jit(solution)/shard_map/dot_general | solution.py:33
  265.4 15.0 %convolution_bitcast_fusion.6 = f32[256,2048]{1,0:T(8,128)S(1)} fusion(bf16[256,512]{1,0:T(8,128)(2,1)S(1)} %bitcast.201, f32[2048,512]{1,0:T(8,128)S(1)} %copy-done.4), kind=kOutput, calls=%fused_computation.82 | convolution fusion | flops 537919488 | bytes 6553600 | tf_op jit(solution)/shard_map/dot_general | solution.py:34
  280.4 15.3 %convolution_bitcast_fusion.7 = f32[256,2048]{1,0:T(8,128)S(1)} fusion(bf16[256,512]{1,0:T(8,128)(2,1)S(1)} %bitcast.202, f32[2048,512]{1,0:T(8,128)S(1)} %copy-done.4), kind=kOutput, calls=%fused_computation.83 | convolution fusion | flops 537919488 | bytes 6553600 | tf_op jit(solution)/shard_map/dot_general | solution.py:33
  297.7 15.0 %convolution_bitcast_fusion.4 = f32[256,2048]{1,0:T(8,128)S(1)} fusion(bf16[256,512]{1,0:T(8,128)(2,1)S(1)} %bitcast.199, f32[2048,512]{1,0:T(8,128)S(1)} %copy-done.2), kind=kOutput, calls=%fused_computation.80 | convolution fusion | flops 537919488 | bytes 6553600 | tf_op jit(solution)/shard_map/dot_general | solution.py:34
  312.7 14.9 %convolution_bitcast_fusion.5 = f32[256,2048]{1,0:T(8,128)S(1)} fusion(bf16[256,512]{1,0:T(8,128)(2,1)S(1)} %bitcast.200, f32[2048,512]{1,0:T(8,128)S(1)} %copy-done.2), kind=kOutput, calls=%fused_computation.81 | convolution fusion | flops 537919488 | bytes 6553600 | tf_op jit(solution)/shard_map/dot_general | solution.py:33
  329.5 14.0 %convert_bitcast_fusion = f32[2,8,16,8,2048]{4,3,1,2,0:T(8,128)} fusion(bf16[2,16,64,2048]{3,1,0,2:T(8,128)(2,1)} %all-to-all-done), kind=kLoop, calls=%fused_computation.1 | loop fusion | flops 4194304 | bytes 25165824 | tf_op jit(solution)/shard_map/convert_element_type | solution.py:60
  355.4 59.7 %fusion.97 = (f32[2,128,1,2048]{3,2,1,0:T(1,128)}, f32[2,128,1,2048]{3,2,1,0:T(1,128)}, f32[2,128,1,2048]{3,2,1,0:T(1,128)S(1)}, f32[2,128,1,2048]{3,2,1,0:T(1,1...) fusion(f32[2,128,8,2048]{3,2,1,0:T(8,128)} %bitcast.198), kind=kLoop, calls=%fused_computation.221 | loop fusion | bytes 33554432 | tf_op jit(solution)/shard_map/slice | solution.py:84
  448.5 14.0 %fusion.57 = f32[256,512]{1,0:T(8,128)S(1)} fusion(bf16[256,2048]{1,0:T(8,128)(2,1)S(1)} %fusion.39, f32[2048,512]{1,0:T(8,128)S(1)} %copy-done.15), kind=kOutput, calls=%fused_computation.152 | convolution fusion | flops 537919488 | bytes 5767168 | tf_op jit(solution)/shard_map/dot_general | solution.py:44
  462.6 14.2 %fusion.56 = f32[256,512]{1,0:T(8,128)S(1)} fusion(bf16[256,2048]{1,0:T(8,128)(2,1)S(1)} %fusion.39, f32[2048,512]{1,0:T(8,128)S(1)} %copy-done.15), kind=kOutput, calls=%fused_computation.151 | convolution fusion | flops 537919488 | bytes 5767168 | tf_op jit(solution)/shard_map/dot_general | solution.py:43
  479.0 14.0 %fusion.71 = f32[256,512]{1,0:T(8,128)S(1)} fusion(bf16[256,2048]{1,0:T(8,128)(2,1)S(1)} %fusion.32, f32[2048,512]{1,0:T(8,128)S(1)} %copy-done.13), kind=kOutput, calls=%fused_computation.166 | convolution fusion | flops 537919488 | bytes 5767168 | tf_op jit(solution)/shard_map/dot_general | solution.py:44
  509.1 14.0 %fusion.59 = f32[256,512]{1,0:T(8,128)S(1)} fusion(bf16[256,2048]{1,0:T(8,128)(2,1)S(1)} %fusion.38, f32[2048,512]{1,0:T(8,128)S(1)} %copy-done.11), kind=kOutput, calls=%fused_computation.154 | convolution fusion | flops 537919488 | bytes 5767168 | tf_op jit(solution)/shard_map/dot_general | solution.py:44
  523.2 14.2 %fusion.58 = f32[256,512]{1,0:T(8,128)S(1)} fusion(bf16[256,2048]{1,0:T(8,128)(2,1)S(1)} %fusion.38, f32[2048,512]{1,0:T(8,128)S(1)} %copy-done.11), kind=kOutput, calls=%fused_computation.153 | convolution fusion | flops 537919488 | bytes 5767168 | tf_op jit(solution)/shard_map/dot_general | solution.py:43
  539.5 14.0 %fusion.61 = f32[256,512]{1,0:T(8,128)S(1)} fusion(bf16[256,2048]{1,0:T(8,128)(2,1)S(1)} %fusion.37, f32[2048,512]{1,0:T(8,128)S(1)} %copy-done.9), kind=kOutput, calls=%fused_computation.156 | convolution fusion | flops 537919488 | bytes 5767168 | tf_op jit(solution)/shard_map/dot_general | solution.py:44
  569.7 14.0 %fusion.63 = f32[256,512]{1,0:T(8,128)S(1)} fusion(bf16[256,2048]{1,0:T(8,128)(2,1)S(1)} %fusion.36, f32[2048,512]{1,0:T(8,128)S(1)} %copy-done.7), kind=kOutput, calls=%fused_computation.158 | convolution fusion | flops 537919488 | bytes 5767168 | tf_op jit(solution)/shard_map/dot_general | solution.py:44
  583.7 14.2 %fusion.62 = f32[256,512]{1,0:T(8,128)S(1)} fusion(bf16[256,2048]{1,0:T(8,128)(2,1)S(1)} %fusion.36, f32[2048,512]{1,0:T(8,128)S(1)} %copy-done.7), kind=kOutput, calls=%fused_computation.157 | convolution fusion | flops 537919488 | bytes 5767168 | tf_op jit(solution)/shard_map/dot_general | solution.py:43
  630.2 14.0 %fusion.67 = f32[256,512]{1,0:T(8,128)S(1)} fusion(bf16[256,2048]{1,0:T(8,128)(2,1)S(1)} %fusion.34, f32[2048,512]{1,0:T(8,128)S(1)} %copy-done.3), kind=kOutput, calls=%fused_computation.162 | convolution fusion | flops 537919488 | bytes 5767168 | tf_op jit(solution)/shard_map/dot_general | solution.py:44
  644.3 14.0 %fusion.66 = f32[256,512]{1,0:T(8,128)S(1)} fusion(bf16[256,2048]{1,0:T(8,128)(2,1)S(1)} %fusion.34, f32[2048,512]{1,0:T(8,128)S(1)} %copy-done.3), kind=kOutput, calls=%fused_computation.161 | convolution fusion | flops 537919488 | bytes 5767168 | tf_op jit(solution)/shard_map/dot_general | solution.py:43
  666.0 86.9 %all-reduce.3.cloned.1.call-done = f32[8,2,128,512]{3,2,1,0:T(8,128)} async-done(((f32[8,2,128,512]{3,2,1,0:T(8,128)}), f32[8,2,128,512]{3,2,1,0:T(8,128)}) %all-reduce.3.cloned.1.call-update) | async-done | bytes 4194320 | tf_op jit(solution)/shard_map/psum | solution.py:91
  755.7 70.3 %all-reduce.5.cloned.1.call-done = f32[128,128]{1,0:T(8,128)} async-done(((f32[128,128]{1,0:T(8,128)}), f32[128,128]{1,0:T(8,128)}) %all-reduce.5.cloned.1.call-update) | async-done | bytes 65552 | tf_op jit(solution)/shard_map/psum | solution.py:97
  (152 shorter events, 174.1 us)
Async XLA Ops:
  7.2 27.5 %copy-start = (s32[64,512]{1,0:T(8,128)S(1)}, s32[64,512]{1,0:T(8,128)}, u32[]{:S(2)}) copy-start(s32[64,512]{1,0:T(8,128)} %param.12) | copy-start | bytes 393220
  7.2 63.1 %all-gather.2.cloned.1.call-start = ((), (), s32[]{:S(2)}) async-start(), calls=%async_computation.1 | async-start | bytes 2621440 | tf_op jit(solution)/shard_map/all_gather | solution.py:62
  26.6 8.0 copy-start.34
  26.6 8.1 copy-start.36
  26.6 8.1 copy-start.35
  26.6 302.9 %all-to-all-start = ((bf16[2,16,64,2048]{3,1,0,2:T(8,128)(2,1)}), bf16[2,16,64,2048]{3,1,0,2:T(8,128)(2,1)}, u32[]{:S(2)}, u32[]{:S(2)}) async-start(bf16[2,16,64,2048]{3,1,0,2:T(8,128)(2,1)} %copy.25), calls=%async_computation | async-start | bytes 16777216 | tf_op jit(solution)/shard_map/all_to_all | solution.py:58
  34.0 719.0 %all-reduce.3.cloned.1.call-start = ((), (), s32[]{:S(2)}) async-start(), calls=%async_computation.2 | async-start | bytes 8388608 | tf_op jit(solution)/shard_map/psum | solution.py:91
  121.0 16.9 %copy-start.12 = (f32[2048,512]{1,0:T(8,128)S(1)}, f32[2048,512]{1,0:T(8,128)}, u32[]{:S(2)}) copy-start(f32[2048,512]{1,0:T(8,128)} %get-tuple-element.12) | copy-start | bytes 12582916
  152.9 16.9 %copy-start.10 = (f32[2048,512]{1,0:T(8,128)S(1)}, f32[2048,512]{1,0:T(8,128)}, u32[]{:S(2)}) copy-start(f32[2048,512]{1,0:T(8,128)} %get-tuple-element.13) | copy-start | bytes 12582916
  184.9 16.7 %copy-start.8 = (f32[2048,512]{1,0:T(8,128)S(1)}, f32[2048,512]{1,0:T(8,128)}, u32[]{:S(2)}) copy-start(f32[2048,512]{1,0:T(8,128)} %get-tuple-element.14) | copy-start | bytes 12582916
  216.8 16.8 %copy-start.6 = (f32[2048,512]{1,0:T(8,128)S(1)}, f32[2048,512]{1,0:T(8,128)}, u32[]{:S(2)}) copy-start(f32[2048,512]{1,0:T(8,128)} %get-tuple-element.15) | copy-start | bytes 12582916
  248.6 16.8 %copy-start.4 = (f32[2048,512]{1,0:T(8,128)S(1)}, f32[2048,512]{1,0:T(8,128)}, u32[]{:S(2)}) copy-start(f32[2048,512]{1,0:T(8,128)} %get-tuple-element.16) | copy-start | bytes 12582916
  280.4 17.2 %copy-start.2 = (f32[2048,512]{1,0:T(8,128)S(1)}, f32[2048,512]{1,0:T(8,128)}, u32[]{:S(2)}) copy-start(f32[2048,512]{1,0:T(8,128)} %get-tuple-element.17) | copy-start | bytes 12582916
  415.1 3.4 copy-start.17
  432.4 13.9 %copy-start.24 = (f32[2,128,1,2048]{3,2,1,0:T(1,128)S(1)}, f32[2,128,1,2048]{3,2,1,0:T(1,128)}, u32[]{:S(2)}) copy-start(f32[2,128,1,2048]{3,2,1,0:T(1,128)} %get-tuple-element.11) | copy-start | bytes 6291460
  432.4 14.9 %copy-start.26 = (f32[2,128,2048]{2,1,0:T(8,128)S(1)}, f32[2,128,2048]{2,1,0:T(8,128)}, u32[]{:S(2)}) copy-start(f32[2,128,2048]{2,1,0:T(8,128)} %maximum_multiply_fusion) | copy-start | bytes 6291460
  462.6 14.2 %copy-start.23 = (f32[2,128,1,2048]{3,2,1,0:T(1,128)S(1)}, f32[2,128,1,2048]{3,2,1,0:T(1,128)}, u32[]{:S(2)}) copy-start(f32[2,128,1,2048]{3,2,1,0:T(1,128)} %get-tuple-element.4) | copy-start | bytes 6291460
  462.6 15.1 %copy-start.27 = (f32[2,128,2048]{2,1,0:T(8,128)S(1)}, f32[2,128,2048]{2,1,0:T(8,128)}, u32[]{:S(2)}) copy-start(f32[2,128,2048]{2,1,0:T(8,128)} %maximum_multiply_fusion.7) | copy-start | bytes 6291460
  492.9 13.9 %copy-start.22 = (f32[2,128,1,2048]{3,2,1,0:T(1,128)S(1)}, f32[2,128,1,2048]{3,2,1,0:T(1,128)}, u32[]{:S(2)}) copy-start(f32[2,128,1,2048]{3,2,1,0:T(1,128)} %get-tuple-element.10) | copy-start | bytes 6291460
  493.0 14.9 %copy-start.28 = (f32[2,128,2048]{2,1,0:T(8,128)S(1)}, f32[2,128,2048]{2,1,0:T(8,128)}, u32[]{:S(2)}) copy-start(f32[2,128,2048]{2,1,0:T(8,128)} %maximum_multiply_fusion.1) | copy-start | bytes 6291460
  523.1 14.2 %copy-start.21 = (f32[2,128,1,2048]{3,2,1,0:T(1,128)S(1)}, f32[2,128,1,2048]{3,2,1,0:T(1,128)}, u32[]{:S(2)}) copy-start(f32[2,128,1,2048]{3,2,1,0:T(1,128)} %get-tuple-element.9) | copy-start | bytes 6291460
  523.2 15.1 %copy-start.29 = (f32[2,128,2048]{2,1,0:T(8,128)S(1)}, f32[2,128,2048]{2,1,0:T(8,128)}, u32[]{:S(2)}) copy-start(f32[2,128,2048]{2,1,0:T(8,128)} %maximum_multiply_fusion.2) | copy-start | bytes 6291460
  553.5 13.9 %copy-start.20 = (f32[2,128,1,2048]{3,2,1,0:T(1,128)S(1)}, f32[2,128,1,2048]{3,2,1,0:T(1,128)}, u32[]{:S(2)}) copy-start(f32[2,128,1,2048]{3,2,1,0:T(1,128)} %get-tuple-element.8) | copy-start | bytes 6291460
  553.5 14.9 %copy-start.30 = (f32[2,128,2048]{2,1,0:T(8,128)S(1)}, f32[2,128,2048]{2,1,0:T(8,128)}, u32[]{:S(2)}) copy-start(f32[2,128,2048]{2,1,0:T(8,128)} %maximum_multiply_fusion.3) | copy-start | bytes 6291460
  583.7 14.2 %copy-start.19 = (f32[2,128,1,2048]{3,2,1,0:T(1,128)S(1)}, f32[2,128,1,2048]{3,2,1,0:T(1,128)}, u32[]{:S(2)}) copy-start(f32[2,128,1,2048]{3,2,1,0:T(1,128)} %get-tuple-element.7) | copy-start | bytes 6291460
  583.7 15.1 %copy-start.31 = (f32[2,128,2048]{2,1,0:T(8,128)S(1)}, f32[2,128,2048]{2,1,0:T(8,128)}, u32[]{:S(2)}) copy-start(f32[2,128,2048]{2,1,0:T(8,128)} %maximum_multiply_fusion.4) | copy-start | bytes 6291460
  614.1 14.8 %copy-start.32 = (f32[2,128,2048]{2,1,0:T(8,128)S(1)}, f32[2,128,2048]{2,1,0:T(8,128)}, u32[]{:S(2)}) copy-start(f32[2,128,2048]{2,1,0:T(8,128)} %maximum_multiply_fusion.5) | copy-start | bytes 6291460
  662.4 90.5 %copy-start.18 = (f32[8,2,128,128]{3,2,1,0:T(8,128)S(1)}, f32[8,2,128,128]{3,2,1,0:T(8,128)}, u32[]{:S(2)}) copy-start(f32[8,2,128,128]{3,2,1,0:T(8,128)} %param.10) | copy-start | bytes 3145732
  664.1 90.9 %copy-start.37 = (f32[128]{0:T(128)S(1)}, f32[128]{0:T(128)}, u32[]{:S(2)}) copy-start(f32[128]{0:T(128)} %param.16) | copy-start | bytes 1540
  664.1 162.7 %copy-start.33 = (f32[8,2,128,128]{3,2,1,0:T(8,128)S(1)}, f32[8,2,128,128]{3,2,1,0:T(8,128)}, u32[]{:S(2)}) copy-start(f32[8,2,128,128]{3,2,1,0:T(8,128)} %param.11) | copy-start | bytes 3145732
  666.0 163.7 %copy-start.1 = (s32[64,512]{1,0:T(8,128)S(1)}, s32[64,512]{1,0:T(8,128)}, u32[]{:S(2)}) copy-start(s32[64,512]{1,0:T(8,128)} %param.12) | copy-start | bytes 393220
  666.0 160.0 %all-reduce.5.cloned.1.call-start = ((), (), s32[]{:S(2)}) async-start(), calls=%async_computation.3 | async-start | bytes 131072 | tf_op jit(solution)/shard_map/psum | solution.py:97
  (10 other events, 23.8 us)
Sparse Core Ops, SparseCore 0:
  10.1 25.5 all-gather.1
  666.1 86.8 all-reduce.2
  757.3 68.6 all-reduce.4
where the time goes:
time: 841 us; the launch traced here: 837 us
  matrix products  464 us (55%)
  waiting for transfers between devices  157 us (19%)
  local copies, waits for them, and re-layouts  118 us (14%)
  other arithmetic  73.5 us (9%)
  between operations  16 us (2%)
    dot_general x8, matrix products, forward_terms(): lax.dot_general(stacked, sin_part, contract, preferred_element_type=jnp.f...  120 us
    dot_general x8, matrix products, forward_terms(): lax.dot_general(stacked, cos_part, contract, preferred_element_type=jnp.f...  120 us
    dot_general x8, matrix products, adjoint_terms(): with_cos = jnp.dot(stacked, cos_part, preferred_element_type=jnp.float32)  112 us
    dot_general x8, matrix products, adjoint_terms(): with_sin = jnp.dot(stacked, sin_part, preferred_element_type=jnp.float32)  112 us
    psum x1, waiting for transfers between devices, local(): summed = lax.psum(partial_sums, 'sta')  86.9 us
    psum x1, waiting for transfers between devices, local(): group_norm = jnp.sqrt(lax.psum(squares, 'freq') + 1e-06)  70.3 us
    slice x1, local copies, waits for them, and re-layouts, local(): relaid[:, :, bin_index, :]  59.7 us
    unnamed x85, local copies, waits for them, and re-layouts  35.6 us
  transfers between devices with their start and end apart: 4, of which 2 were waited for; matrix products, arithmetic and copies ran while one was open for 37% of the time, Pallas kernels for 0%

commit v1 on v0

--- a/solution.py
+++ b/solution.py
@@ -6,6 +6,15 @@
 
 F = 64
 CELLS = 512
+
+
+def sum_by_hops(x, mesh_axis):
+    size = lax.axis_size(mesh_axis)
+    total, far = (x, 1)
+    while far < size:
+        total = total + lax.ppermute(total, mesh_axis, [(i, i ^ far) for i in range(size)])
+        far = 2 * far
+    return total
 
 
 def cell_block(cell_count):
@@ -88,7 +97,7 @@
             adjoint_terms(cos_all[bin_index], sin_all[bin_index], residual) * normalizer
         )
     partial_sums = jnp.stack(bin_sums)
-    summed = lax.psum(partial_sums, "sta")
+    summed = sum_by_hops(partial_sums, "sta")
     gradient = lax.dynamic_slice_in_dim(summed, lax.axis_index("sta") * cell_share, cell_share, 3)
     step_size = CELLS / (math.sqrt(station_total) + math.sqrt(CELLS)) ** 2
     stepped = current - step_size * gradient

time: 841 us -> 849 us (level)
  waiting for transfers between devices: 157 us -> 168 us
    ppermute x0 -> x2, waiting for transfers between devices: none -> 98.6 us  [sum_by_hops(): lax.ppermute(total, mesh_axis, [(i, i ^ far) for i in range(size)])]
    psum x1 -> x0, waiting for transfers between devices: 86.9 us -> none  [local(): summed = lax.psum(partial_sums, 'sta')]
  transfers between devices with their start and end apart: 4 -> 5, of which waited for: 2 -> 3; matrix products, arithmetic and copies ran while one was open for 37% -> 37% of each run, Pallas kernels for 0% -> 0%
where the time goes in v1:
time: 849 us; the launch traced here: 845 us
  matrix products  464 us (55%)
  waiting for transfers between devices  168 us (20%)
  local copies, waits for them, and re-layouts  118 us (14%)
  other arithmetic  69.1 us (8%)
  between operations  16.3 us (2%)
  starting transfers between devices  9.58 us (1%)
    dot_general x8, matrix products, forward_terms(): lax.dot_general(stacked, sin_part, contract, preferred_element_type=jnp.f...  120 us
    dot_general x8, matrix products, forward_terms(): lax.dot_general(stacked, cos_part, contract, preferred_element_type=jnp.f...  120 us
    dot_general x8, matrix products, adjoint_terms(): with_cos = jnp.dot(stacked, cos_part, preferred_element_type=jnp.float32)  112 us
    dot_general x8, matrix products, adjoint_terms(): with_sin = jnp.dot(stacked, sin_part, preferred_element_type=jnp.float32)  112 us
    ppermute x2, waiting for transfers between devices, sum_by_hops(): lax.ppermute(total, mesh_axis, [(i, i ^ far) for i in range(size)])  98.6 us
    psum x1, waiting for transfers between devices, local(): group_norm = jnp.sqrt(lax.psum(squares, 'freq') + 1e-06)  69.2 us
    slice x1, local copies, waits for them, and re-layouts, local(): relaid[:, :, bin_index, :]  59.7 us
    unnamed x85, local copies, waits for them, and re-layouts  35.6 us
  transfers between devices with their start and end apart: 5, of which 3 were waited for; matrix products, arithmetic and copies ran while one was open for 37% of the time, Pallas kernels for 0%

profile of v1, /device:TPU:0, one launch (start us, length us, event | category | flops | bytes accessed | tf_op | source)
XLA Modules:
  0.0 844.7 jit_solution(14998210597299377707)
XLA Ops:
  9.4 17.2 %copy.25 = bf16[2,16,64,2048]{3,1,0,2:T(8,128)(2,1)} copy(f32[2,16,64,2048]{3,2,1,0:T(8,128)} %param.9) | data formatting | bytes 25165824 | tf_op args[0]
  43.6 18.0 %fusion.31 = (f32[2048,512]{1,0:T(8,128)}, f32[2048,512]{1,0:T(8,128)}, f32[2048,512]{1,0:T(8,128)}, f32[2048,512]{1,0:T(8,128)}, f32[2048,512]{1,0:T(8,128)}, /*index=5*/f32[2048,512]{1,0:T(8,128)}) fusion(s32[2048,512]{1,0:T(8,128)} %gather_fusion, f32[]{:T(128)S(6)} %convert_element_type.188, s32[]{:T(128)S(6)} %add.234, f32[512]{0:T(512)S(1)} %bitcast.221, ...), kind=kLoop, calls=%fused_computation.58 | loop fusion | flops 104857600 | bytes 29382704 | tf_op jit(solution)/shard_map/mul | solution.py:32
  73.1 15.0 %convolution_bitcast_fusion.2 = f32[256,2048]{1,0:T(8,128)S(1)} fusion(bf16[256,512]{1,0:T(8,128)(2,1)S(1)} %bitcast.213, f32[2048,512]{1,0:T(8,128)S(1)} %copy-done.16), kind=kOutput, calls=%fused_computation.78 | convolution fusion | flops 537919488 | bytes 6553600 | tf_op jit(solution)/shard_map/dot_general | solution.py:43
  88.1 14.9 %convolution_bitcast_fusion.3 = f32[256,2048]{1,0:T(8,128)S(1)} fusion(bf16[256,512]{1,0:T(8,128)(2,1)S(1)} %bitcast.214, f32[2048,512]{1,0:T(8,128)S(1)} %copy-done.16), kind=kOutput, calls=%fused_computation.79 | convolution fusion | flops 537919488 | bytes 6553600 | tf_op jit(solution)/shard_map/dot_general | solution.py:42
  105.9 15.0 %convolution_bitcast_fusion.14 = f32[256,2048]{1,0:T(8,128)S(1)} fusion(bf16[256,512]{1,0:T(8,128)(2,1)S(1)} %bitcast.211, f32[2048,512]{1,0:T(8,128)S(1)} %copy-done.14), kind=kOutput, calls=%fused_computation.90 | convolution fusion | flops 537919488 | bytes 6553600 | tf_op jit(solution)/shard_map/dot_general | solution.py:43
  121.0 15.1 %convolution_bitcast_fusion.15 = f32[256,2048]{1,0:T(8,128)S(1)} fusion(bf16[256,512]{1,0:T(8,128)(2,1)S(1)} %bitcast.212, f32[2048,512]{1,0:T(8,128)S(1)} %copy-done.14), kind=kOutput, calls=%fused_computation.91 | convolution fusion | flops 537919488 | bytes 6553600 | tf_op jit(solution)/shard_map/dot_general | solution.py:42
  137.9 15.0 %convolution_bitcast_fusion = f32[256,2048]{1,0:T(8,128)S(1)} fusion(bf16[256,512]{1,0:T(8,128)(2,1)S(1)} %bitcast.209, f32[2048,512]{1,0:T(8,128)S(1)} %copy-done.12), kind=kOutput, calls=%fused_computation.76 | convolution fusion | flops 537919488 | bytes 6553600 | tf_op jit(solution)/shard_map/dot_general | solution.py:43
  152.9 14.9 %convolution_bitcast_fusion.1 = f32[256,2048]{1,0:T(8,128)S(1)} fusion(bf16[256,512]{1,0:T(8,128)(2,1)S(1)} %bitcast.210, f32[2048,512]{1,0:T(8,128)S(1)} %copy-done.12), kind=kOutput, calls=%fused_computation.77 | convolution fusion | flops 537919488 | bytes 6553600 | tf_op jit(solution)/shard_map/dot_general | solution.py:42
  169.8 15.0 %convolution_bitcast_fusion.12 = f32[256,2048]{1,0:T(8,128)S(1)} fusion(bf16[256,512]{1,0:T(8,128)(2,1)S(1)} %bitcast.207, f32[2048,512]{1,0:T(8,128)S(1)} %copy-done.10), kind=kOutput, calls=%fused_computation.88 | convolution fusion | flops 537919488 | bytes 6553600 | tf_op jit(solution)/shard_map/dot_general | solution.py:43
  184.8 14.9 %convolution_bitcast_fusion.13 = f32[256,2048]{1,0:T(8,128)S(1)} fusion(bf16[256,512]{1,0:T(8,128)(2,1)S(1)} %bitcast.208, f32[2048,512]{1,0:T(8,128)S(1)} %copy-done.10), kind=kOutput, calls=%fused_computation.89 | convolution fusion | flops 537919488 | bytes 6553600 | tf_op jit(solution)/shard_map/dot_general | solution.py:42
  201.6 15.2 %convolution_bitcast_fusion.10 = f32[256,2048]{1,0:T(8,128)S(1)} fusion(bf16[256,512]{1,0:T(8,128)(2,1)S(1)} %bitcast.205, f32[2048,512]{1,0:T(8,128)S(1)} %copy-done.8), kind=kOutput, calls=%fused_computation.86 | convolution fusion | flops 537919488 | bytes 6553600 | tf_op jit(solution)/shard_map/dot_general | solution.py:43
  216.8 14.9 %convolution_bitcast_fusion.11 = f32[256,2048]{1,0:T(8,128)S(1)} fusion(bf16[256,512]{1,0:T(8,128)(2,1)S(1)} %bitcast.206, f32[2048,512]{1,0:T(8,128)S(1)} %copy-done.8), kind=kOutput, calls=%fused_computation.87 | convolution fusion | flops 537919488 | bytes 6553600 | tf_op jit(solution)/shard_map/dot_general | solution.py:42
  233.6 15.0 %convolution_bitcast_fusion.8 = f32[256,2048]{1,0:T(8,128)S(1)} fusion(bf16[256,512]{1,0:T(8,128)(2,1)S(1)} %bitcast.203, f32[2048,512]{1,0:T(8,128)S(1)} %copy-done.6), kind=kOutput, calls=%fused_computation.84 | convolution fusion | flops 537919488 | bytes 6553600 | tf_op jit(solution)/shard_map/dot_general | solution.py:43
  248.6 14.9 %convolution_bitcast_fusion.9 = f32[256,2048]{1,0:T(8,128)S(1)} fusion(bf16[256,512]{1,0:T(8,128)(2,1)S(1)} %bitcast.204, f32[2048,512]{1,0:T(8,128)S(1)} %copy-done.6), kind=kOutput, calls=%fused_computation.85 | convolution fusion | flops 537919488 | bytes 6553600 | tf_op jit(solution)/shard_map/dot_general | solution.py:42
  265.4 15.0 %convolution_bitcast_fusion.6 = f32[256,2048]{1,0:T(8,128)S(1)} fusion(bf16[256,512]{1,0:T(8,128)(2,1)S(1)} %bitcast.201, f32[2048,512]{1,0:T(8,128)S(1)} %copy-done.4), kind=kOutput, calls=%fused_computation.82 | convolution fusion | flops 537919488 | bytes 6553600 | tf_op jit(solution)/shard_map/dot_general | solution.py:43
  280.4 15.3 %convolution_bitcast_fusion.7 = f32[256,2048]{1,0:T(8,128)S(1)} fusion(bf16[256,512]{1,0:T(8,128)(2,1)S(1)} %bitcast.202, f32[2048,512]{1,0:T(8,128)S(1)} %copy-done.4), kind=kOutput, calls=%fused_computation.83 | convolution fusion | flops 537919488 | bytes 6553600 | tf_op jit(solution)/shard_map/dot_general | solution.py:42
  297.6 15.0 %convolution_bitcast_fusion.4 = f32[256,2048]{1,0:T(8,128)S(1)} fusion(bf16[256,512]{1,0:T(8,128)(2,1)S(1)} %bitcast.199, f32[2048,512]{1,0:T(8,128)S(1)} %copy-done.2), kind=kOutput, calls=%fused_computation.80 | convolution fusion | flops 537919488 | bytes 6553600 | tf_op jit(solution)/shard_map/dot_general | solution.py:43
  312.6 14.9 %convolution_bitcast_fusion.5 = f32[256,2048]{1,0:T(8,128)S(1)} fusion(bf16[256,512]{1,0:T(8,128)(2,1)S(1)} %bitcast.200, f32[2048,512]{1,0:T(8,128)S(1)} %copy-done.2), kind=kOutput, calls=%fused_computation.81 | convolution fusion | flops 537919488 | bytes 6553600 | tf_op jit(solution)/shard_map/dot_general | solution.py:42
  329.4 14.0 %convert_bitcast_fusion = f32[2,8,16,8,2048]{4,3,1,2,0:T(8,128)} fusion(bf16[2,16,64,2048]{3,1,0,2:T(8,128)(2,1)} %all-to-all-done), kind=kLoop, calls=%fused_computation.1 | loop fusion | flops 4194304 | bytes 25165824 | tf_op jit(solution)/shard_map/convert_element_type | solution.py:69
  355.3 59.7 %fusion.100 = (f32[2,128,1,2048]{3,2,1,0:T(1,128)}, f32[2,128,1,2048]{3,2,1,0:T(1,128)}, f32[2,128,1,2048]{3,2,1,0:T(1,128)S(1)}, f32[2,128,1,2048]{3,2,1,0:T(1,...) fusion(f32[2,128,8,2048]{3,2,1,0:T(8,128)} %bitcast.198), kind=kLoop, calls=%fused_computation.223 | loop fusion | bytes 33554432 | tf_op jit(solution)/shard_map/slice | solution.py:93
  448.4 14.0 %fusion.59 = f32[256,512]{1,0:T(8,128)S(1)} fusion(bf16[256,2048]{1,0:T(8,128)(2,1)S(1)} %fusion.39, f32[2048,512]{1,0:T(8,128)S(1)} %copy-done.15), kind=kOutput, calls=%fused_computation.154 | convolution fusion | flops 537919488 | bytes 5767168 | tf_op jit(solution)/shard_map/dot_general | solution.py:53
  462.5 14.2 %fusion.58 = f32[256,512]{1,0:T(8,128)S(1)} fusion(bf16[256,2048]{1,0:T(8,128)(2,1)S(1)} %fusion.39, f32[2048,512]{1,0:T(8,128)S(1)} %copy-done.15), kind=kOutput, calls=%fused_computation.153 | convolution fusion | flops 537919488 | bytes 5767168 | tf_op jit(solution)/shard_map/dot_general | solution.py:52
  478.9 14.0 %fusion.73 = f32[256,512]{1,0:T(8,128)S(1)} fusion(bf16[256,2048]{1,0:T(8,128)(2,1)S(1)} %fusion.32, f32[2048,512]{1,0:T(8,128)S(1)} %copy-done.13), kind=kOutput, calls=%fused_computation.168 | convolution fusion | flops 537919488 | bytes 5767168 | tf_op jit(solution)/shard_map/dot_general | solution.py:53
  509.0 14.0 %fusion.61 = f32[256,512]{1,0:T(8,128)S(1)} fusion(bf16[256,2048]{1,0:T(8,128)(2,1)S(1)} %fusion.38, f32[2048,512]{1,0:T(8,128)S(1)} %copy-done.11), kind=kOutput, calls=%fused_computation.156 | convolution fusion | flops 537919488 | bytes 5767168 | tf_op jit(solution)/shard_map/dot_general | solution.py:53
  523.1 14.2 %fusion.60 = f32[256,512]{1,0:T(8,128)S(1)} fusion(bf16[256,2048]{1,0:T(8,128)(2,1)S(1)} %fusion.38, f32[2048,512]{1,0:T(8,128)S(1)} %copy-done.11), kind=kOutput, calls=%fused_computation.155 | convolution fusion | flops 537919488 | bytes 5767168 | tf_op jit(solution)/shard_map/dot_general | solution.py:52
  539.4 14.0 %fusion.63 = f32[256,512]{1,0:T(8,128)S(1)} fusion(bf16[256,2048]{1,0:T(8,128)(2,1)S(1)} %fusion.37, f32[2048,512]{1,0:T(8,128)S(1)} %copy-done.9), kind=kOutput, calls=%fused_computation.158 | convolution fusion | flops 537919488 | bytes 5767168 | tf_op jit(solution)/shard_map/dot_general | solution.py:53
  569.6 14.0 %fusion.65 = f32[256,512]{1,0:T(8,128)S(1)} fusion(bf16[256,2048]{1,0:T(8,128)(2,1)S(1)} %fusion.36, f32[2048,512]{1,0:T(8,128)S(1)} %copy-done.7), kind=kOutput, calls=%fused_computation.160 | convolution fusion | flops 537919488 | bytes 5767168 | tf_op jit(solution)/shard_map/dot_general | solution.py:53
  583.6 14.2 %fusion.64 = f32[256,512]{1,0:T(8,128)S(1)} fusion(bf16[256,2048]{1,0:T(8,128)(2,1)S(1)} %fusion.36, f32[2048,512]{1,0:T(8,128)S(1)} %copy-done.7), kind=kOutput, calls=%fused_computation.159 | convolution fusion | flops 537919488 | bytes 5767168 | tf_op jit(solution)/shard_map/dot_general | solution.py:52
  630.1 14.0 %fusion.69 = f32[256,512]{1,0:T(8,128)S(1)} fusion(bf16[256,2048]{1,0:T(8,128)(2,1)S(1)} %fusion.34, f32[2048,512]{1,0:T(8,128)S(1)} %copy-done.3), kind=kOutput, calls=%fused_computation.164 | convolution fusion | flops 537919488 | bytes 5767168 | tf_op jit(solution)/shard_map/dot_general | solution.py:53
  644.2 14.0 %fusion.68 = f32[256,512]{1,0:T(8,128)S(1)} fusion(bf16[256,2048]{1,0:T(8,128)(2,1)S(1)} %fusion.34, f32[2048,512]{1,0:T(8,128)S(1)} %copy-done.3), kind=kOutput, calls=%fused_computation.163 | convolution fusion | flops 537919488 | bytes 5767168 | tf_op jit(solution)/shard_map/dot_general | solution.py:52
  671.1 91.4 %collective-permute-done.1 = f32[8,2,128,512]{3,2,1,0:T(8,128)} collective-permute-done((f32[8,2,128,512]{3,2,1,0:T(8,128)}, f32[8,2,128,512]{3,2,1,0:T(8,128)}, u32[]{:S(2)}, u32[]{:S(2)}) %collective-permute-start.1) | collective-permute-done | bytes 4194336 | tf_op jit(solution)/shard_map/ppermute | solution.py:15
  765.7 69.2 %all-reduce.2.cloned.1.call-done = f32[128,128]{1,0:T(8,128)} async-done(((f32[128,128]{1,0:T(8,128)}), f32[128,128]{1,0:T(8,128)}) %all-reduce.2.cloned.1.call-update) | async-done | bytes 65552 | tf_op jit(solution)/shard_map/psum | solution.py:106
  (154 shorter events, 178.3 us)
Async XLA Ops:
  7.2 27.5 %copy-start = (s32[64,512]{1,0:T(8,128)S(1)}, s32[64,512]{1,0:T(8,128)}, u32[]{:S(2)}) copy-start(s32[64,512]{1,0:T(8,128)} %param.12) | copy-start | bytes 393220
  7.2 63.1 %all-gather.2.cloned.1.call-start = ((), (), s32[]{:S(2)}) async-start(), calls=%async_computation.1 | async-start | bytes 2621440 | tf_op jit(solution)/shard_map/all_gather | solution.py:71
  26.6 8.0 copy-start.34
  26.6 8.1 copy-start.36
  26.6 8.1 copy-start.35
  26.6 302.8 %all-to-all-start = ((bf16[2,16,64,2048]{3,1,0,2:T(8,128)(2,1)}), bf16[2,16,64,2048]{3,1,0,2:T(8,128)(2,1)}, u32[]{:S(2)}, u32[]{:S(2)}) async-start(bf16[2,16,64,2048]{3,1,0,2:T(8,128)(2,1)} %copy.25), calls=%async_computation | async-start | bytes 16777216 | tf_op jit(solution)/shard_map/all_to_all | solution.py:67
  34.0 801.0 %all-reduce.2.cloned.1.call-start = ((), (), s32[]{:S(2)}) async-start(), calls=%async_computation.2 | async-start | bytes 131072 | tf_op jit(solution)/shard_map/psum | solution.py:106
  120.9 16.9 %copy-start.12 = (f32[2048,512]{1,0:T(8,128)S(1)}, f32[2048,512]{1,0:T(8,128)}, u32[]{:S(2)}) copy-start(f32[2048,512]{1,0:T(8,128)} %get-tuple-element.14) | copy-start | bytes 12582916
  152.9 16.9 %copy-start.10 = (f32[2048,512]{1,0:T(8,128)S(1)}, f32[2048,512]{1,0:T(8,128)}, u32[]{:S(2)}) copy-start(f32[2048,512]{1,0:T(8,128)} %get-tuple-element.15) | copy-start | bytes 12582916
  184.8 16.7 %copy-start.8 = (f32[2048,512]{1,0:T(8,128)S(1)}, f32[2048,512]{1,0:T(8,128)}, u32[]{:S(2)}) copy-start(f32[2048,512]{1,0:T(8,128)} %get-tuple-element.16) | copy-start | bytes 12582916
  216.8 16.8 %copy-start.6 = (f32[2048,512]{1,0:T(8,128)S(1)}, f32[2048,512]{1,0:T(8,128)}, u32[]{:S(2)}) copy-start(f32[2048,512]{1,0:T(8,128)} %get-tuple-element.17) | copy-start | bytes 12582916
  248.6 16.8 %copy-start.4 = (f32[2048,512]{1,0:T(8,128)S(1)}, f32[2048,512]{1,0:T(8,128)}, u32[]{:S(2)}) copy-start(f32[2048,512]{1,0:T(8,128)} %get-tuple-element.18) | copy-start | bytes 12582916
  280.4 17.2 %copy-start.2 = (f32[2048,512]{1,0:T(8,128)S(1)}, f32[2048,512]{1,0:T(8,128)}, u32[]{:S(2)}) copy-start(f32[2048,512]{1,0:T(8,128)} %get-tuple-element.19) | copy-start | bytes 12582916
  432.3 13.9 %copy-start.23 = (f32[2,128,1,2048]{3,2,1,0:T(1,128)S(1)}, f32[2,128,1,2048]{3,2,1,0:T(1,128)}, u32[]{:S(2)}) copy-start(f32[2,128,1,2048]{3,2,1,0:T(1,128)} %get-tuple-element.13) | copy-start | bytes 6291460
  432.3 14.9 %copy-start.25 = (f32[2,128,2048]{2,1,0:T(8,128)S(1)}, f32[2,128,2048]{2,1,0:T(8,128)}, u32[]{:S(2)}) copy-start(f32[2,128,2048]{2,1,0:T(8,128)} %maximum_multiply_fusion) | copy-start | bytes 6291460
  462.5 14.2 %copy-start.22 = (f32[2,128,1,2048]{3,2,1,0:T(1,128)S(1)}, f32[2,128,1,2048]{3,2,1,0:T(1,128)}, u32[]{:S(2)}) copy-start(f32[2,128,1,2048]{3,2,1,0:T(1,128)} %get-tuple-element.6) | copy-start | bytes 6291460
  462.5 15.1 %copy-start.26 = (f32[2,128,2048]{2,1,0:T(8,128)S(1)}, f32[2,128,2048]{2,1,0:T(8,128)}, u32[]{:S(2)}) copy-start(f32[2,128,2048]{2,1,0:T(8,128)} %maximum_multiply_fusion.7) | copy-start | bytes 6291460
  492.9 13.9 %copy-start.21 = (f32[2,128,1,2048]{3,2,1,0:T(1,128)S(1)}, f32[2,128,1,2048]{3,2,1,0:T(1,128)}, u32[]{:S(2)}) copy-start(f32[2,128,1,2048]{3,2,1,0:T(1,128)} %get-tuple-element.12) | copy-start | bytes 6291460
  492.9 14.9 %copy-start.27 = (f32[2,128,2048]{2,1,0:T(8,128)S(1)}, f32[2,128,2048]{2,1,0:T(8,128)}, u32[]{:S(2)}) copy-start(f32[2,128,2048]{2,1,0:T(8,128)} %maximum_multiply_fusion.1) | copy-start | bytes 6291460
  523.1 14.2 %copy-start.20 = (f32[2,128,1,2048]{3,2,1,0:T(1,128)S(1)}, f32[2,128,1,2048]{3,2,1,0:T(1,128)}, u32[]{:S(2)}) copy-start(f32[2,128,1,2048]{3,2,1,0:T(1,128)} %get-tuple-element.11) | copy-start | bytes 6291460
  523.1 15.1 %copy-start.28 = (f32[2,128,2048]{2,1,0:T(8,128)S(1)}, f32[2,128,2048]{2,1,0:T(8,128)}, u32[]{:S(2)}) copy-start(f32[2,128,2048]{2,1,0:T(8,128)} %maximum_multiply_fusion.2) | copy-start | bytes 6291460
  553.4 13.9 %copy-start.19 = (f32[2,128,1,2048]{3,2,1,0:T(1,128)S(1)}, f32[2,128,1,2048]{3,2,1,0:T(1,128)}, u32[]{:S(2)}) copy-start(f32[2,128,1,2048]{3,2,1,0:T(1,128)} %get-tuple-element.10) | copy-start | bytes 6291460
  553.4 14.9 %copy-start.29 = (f32[2,128,2048]{2,1,0:T(8,128)S(1)}, f32[2,128,2048]{2,1,0:T(8,128)}, u32[]{:S(2)}) copy-start(f32[2,128,2048]{2,1,0:T(8,128)} %maximum_multiply_fusion.3) | copy-start | bytes 6291460
  583.6 14.2 %copy-start.18 = (f32[2,128,1,2048]{3,2,1,0:T(1,128)S(1)}, f32[2,128,1,2048]{3,2,1,0:T(1,128)}, u32[]{:S(2)}) copy-start(f32[2,128,1,2048]{3,2,1,0:T(1,128)} %get-tuple-element.9) | copy-start | bytes 6291460
  583.6 15.1 %copy-start.30 = (f32[2,128,2048]{2,1,0:T(8,128)S(1)}, f32[2,128,2048]{2,1,0:T(8,128)}, u32[]{:S(2)}) copy-start(f32[2,128,2048]{2,1,0:T(8,128)} %maximum_multiply_fusion.4) | copy-start | bytes 6291460
  614.0 14.8 %copy-start.31 = (f32[2,128,2048]{2,1,0:T(8,128)S(1)}, f32[2,128,2048]{2,1,0:T(8,128)}, u32[]{:S(2)}) copy-start(f32[2,128,2048]{2,1,0:T(8,128)} %maximum_multiply_fusion.5) | copy-start | bytes 6291460
  659.4 103.2 %copy-start.32 = (f32[8,2,128,128]{3,2,1,0:T(8,128)S(1)}, f32[8,2,128,128]{3,2,1,0:T(8,128)}, u32[]{:S(2)}) copy-start(f32[8,2,128,128]{3,2,1,0:T(8,128)} %param.10) | copy-start | bytes 3145732
  659.4 7.2 collective-permute-start
  669.6 95.4 %copy-start.37 = (f32[128]{0:T(128)S(1)}, f32[128]{0:T(128)}, u32[]{:S(2)}) copy-start(f32[128]{0:T(128)} %param.16) | copy-start | bytes 1540
  669.6 166.2 %copy-start.33 = (f32[8,2,128,128]{3,2,1,0:T(8,128)S(1)}, f32[8,2,128,128]{3,2,1,0:T(8,128)}, u32[]{:S(2)}) copy-start(f32[8,2,128,128]{3,2,1,0:T(8,128)} %param.11) | copy-start | bytes 3145732
  669.6 92.9 %collective-permute-start.1 = (f32[8,2,128,512]{3,2,1,0:T(8,128)}, f32[8,2,128,512]{3,2,1,0:T(8,128)}, u32[]{:S(2)}, u32[]{:S(2)}) collective-permute-start(f32[8,2,128,512]{3,2,1,0:T(8,128)} %add.239), channel_id=1, source_target_pairs={{0,2},{1,3},{2,0},{3,1},{4,6},{5,7},{6,4},{7,5},{8,10},{9,11},{10,... | collective-permute-start | bytes 12582920 | tf_op jit(solution)/shard_map/ppermute | solution.py:15
  671.1 166.3 %copy-start.1 = (s32[64,512]{1,0:T(8,128)S(1)}, s32[64,512]{1,0:T(8,128)}, u32[]{:S(2)}) copy-start(s32[64,512]{1,0:T(8,128)} %param.12) | copy-start | bytes 393220
  (11 other events, 27.2 us)
Sparse Core Ops, SparseCore 0:
  10.1 25.5 all-gather.1
  765.1 69.8 all-reduce.1
